TPU v7x, 32 devices: a whole 2x2x4 slice. The times are simulated.
32 devices in a mesh: parts: 2 (over y), node: 4 (over z), local: 4 (over x, core).
Axes of the slice: x: 2, y: 2, z: 4, core: 2. Of those that a mesh axis runs over, the one named last changes fastest.
Arguments:
- hidden_states: bfloat16 [8192, 7168], P(('parts', 'node', 'local')), parts along dimension 0, may hold values from -6 to 6
- expert_ids: int32 [8192, 8], P(('parts', 'node', 'local')), parts along dimension 0, may hold values from 0 to 255, as said below
- route_weights: float32 [8192, 8], P(('parts', 'node', 'local')), parts along dimension 0, may hold values from 0.1 to 0.8
- gate_weight: bfloat16 [4, 7168, 2048], P('local', None, 'node'), may hold values from -0.0625 to 0.0625
- up_weight: bfloat16 [4, 7168, 2048], P('local', None, 'node'), may hold values from -0.0625 to 0.0625
- down_weight: bfloat16 [4, 2048, 7168], P('local', 'node'), may hold values from -0.125 to 0.125
Outputs:
- combined: bfloat16 [8192, 7168], P(('parts', 'node', 'local')), parts along dimension 0
There are 2 independent parts, one for each index of `parts`. A program takes and returns all parts, laid end to end along the dimension named above; an argument that names none is the same for every part. Nothing has to cross between parts.
Inputs may be any that keep to these rules, and one draw needn't show every extreme that they name: `expert_ids`: each token names 8 distinct experts. Of the 256 tokens of one device, at most 5 name any one expert f * 64 (f below 4); in every draw one such expert is named by exactly 5 tokens of every device, and on each device some expert reaches 5.
All inputs are finite; a program needn't handle non-finite values.
Results may differ from a plain program's by a relative error of at most 0.01.
Values may be sent and summed in bfloat16 or wider, within the bound.
A program may use at most 128 MiB of HBM per device.

v0:
```python
import jax
import jax.numpy as jnp
from jax import lax
from jax.sharding import PartitionSpec as P

EXPERTS = 256
CAP = 5


def on_device(hidden_states, expert_ids, route_weights, gate_weight, up_weight, down_weight):
    live_count = lax.axis_size("local")
    tok_rows = hidden_states.shape[0]
    model_width = hidden_states.shape[1]
    stride = EXPERTS // live_count
    wanted = jnp.arange(live_count, dtype=jnp.int32) * stride
    matched = expert_ids[:, :, None] == wanted[None, None, :]
    match_any = jnp.any(matched, axis=1).astype(jnp.int32)
    route_share = jnp.sum(jnp.where(matched, route_weights[:, :, None], 0.0), axis=1)
    position = jnp.cumsum(match_any, axis=0) - match_any
    slot_range = jnp.arange(CAP, dtype=jnp.int32)
    selector = (match_any[:, :, None] > 0) & (position[:, :, None] == slot_range[None, None, :])
    send_rows = jnp.einsum(
        "tfc,td->fcd",
        selector.astype(jnp.bfloat16),
        hidden_states,
        preferred_element_type=jnp.float32,
    ).astype(jnp.bfloat16)
    gate_block = gate_weight[0]
    up_block = up_weight[0]
    down_block = down_weight[0]
    gathered = lax.all_gather(send_rows[None], "node", axis=0, tiled=True)
    arrived = lax.all_to_all(gathered, "local", split_axis=1, concat_axis=1, tiled=True)
    flat_rows = arrived.reshape(-1, model_width)
    gate_proj = jnp.dot(flat_rows, gate_block, preferred_element_type=jnp.float32)
    up_proj = jnp.dot(flat_rows, up_block, preferred_element_type=jnp.float32)
    activation = (jax.nn.silu(gate_proj) * up_proj).astype(jnp.bfloat16)
    hidden_act = activation.reshape(arrived.shape[:-1] + (activation.shape[-1],))
    flat_act = hidden_act.reshape(-1, hidden_act.shape[-1])
    summed = lax.psum_scatter(
        jnp.dot(flat_act, down_block, preferred_element_type=jnp.float32).astype(jnp.bfloat16),
        "node",
        scatter_dimension=0,
        tiled=True,
    )
    expert_out = summed.reshape(live_count, CAP, model_width)
    returned = lax.all_to_all(expert_out, "local", split_axis=0, concat_axis=0, tiled=True)
    mixing = (selector.astype(jnp.float32) * route_share[:, :, None]).reshape(
        tok_rows, live_count * CAP
    )
    combined = jnp.dot(
        mixing,
        returned.reshape(-1, model_width).astype(jnp.float32),
        precision=lax.Precision.HIGHEST,
        preferred_element_type=jnp.float32,
    )
    return combined.astype(jnp.bfloat16)


def solution(mesh):
    placed = (
        P(("parts", "node", "local"), None),
        P(("parts", "node", "local"), None),
        P(("parts", "node", "local"), None),
        P("local", None, "node"),
        P("local", None, "node"),
        P("local", "node", None),
    )
    return jax.shard_map(
        on_device,
        mesh=mesh,
        in_specs=placed,
        out_specs=P(("parts", "node", "local"), None),
        check_vma=False,
    )
```

profile of v0, /device:TPU:0, one launch (start us, length us, event | category | flops | bytes accessed | tf_op | source)
XLA Modules:
  0.0 151.7 jit_solution(15349934123690530097)
XLA Ops:
  6.5 0.8 compare_reduce_fusion
  7.4 1.2 reduce-window.6
  8.6 0.1 slice.8
  8.7 0.1 copy.21
  8.8 0.1 copy.22
  8.9 0.1 add_bitcast_fusion
  9.0 3.4 %convolution_convert_fusion.1 = bf16[4,5,7168]{2,1,0:T(8,128)(2,1)} fusion(bf16[256,7168]{1,0:T(8,128)(2,1)} %param.6, s32[256,4]{0,1:T(4,128)S(1)} %convert_subtract_fusion, pred[256,4]{0,1:T(4,128)(4,1)S(1)} %get-tuple-element.5), kind=kOutput, calls=%fused_computation.3 | convolution fusion | flops 73553920 | bytes 3961856 | tf_op jit(solution)/shard_map/tfc,td->fcd/dot_general | solution.py:22
  12.4 0.0 all-gather.3.cloned.1.call-update
  12.4 44.3 %all-gather.3.cloned.1.call-done = bf16[16,5,7168]{2,1,0:T(8,128)(2,1)} async-done(((bf16[4,5,7168]{2,1,0:T(8,128)(2,1)}), bf16[16,5,7168]{2,1,0:T(8,128)(2,1)}) %all-gather.3.cloned.1.call-update) | async-done | bytes 1146896 | tf_op jit(solution)/shard_map/all_gather | solution.py:31
  56.7 2.5 %copy.23 = bf16[4,4,5,7168]{3,0,2,1:T(4,128)(2,1)S(1)} copy(bf16[4,4,5,7168]{3,2,1,0:T(8,128)(2,1)} %bitcast.42) | data formatting | bytes 2293760 | tf_op jit(solution)/shard_map/all_gather | solution.py:31
  59.2 18.1 %all_to_all.10 = bf16[4,4,5,7168]{3,0,2,1:T(4,128)(2,1)S(1)} all-to-all(bf16[4,4,5,7168]{3,0,2,1:T(4,128)(2,1)S(1)} %copy.23), channel_id=1, replica_groups=mesh['parts'=2,'node'=4,'local'=4] {'local'}, dimensions={1} | all-to-all | bytes 2293760 | tf_op jit(solution)/shard_map/all_to_all | solution.py:32
  77.2 0.4 copy.24
  77.7 0.6 reshape.34
  78.3 4.5 %fusion.5 = f32[80,512]{1,0:T(8,128)S(1)} fusion(bf16[80,7168]{1,0:T(8,128)(2,1)S(1)} %reshape.34, bf16[1,7168,512]{2,1,0:T(8,128)(2,1)} %param.9), kind=kOutput, calls=%fused_computation.7 | convolution fusion | flops 587202560 | bytes 8650752 | tf_op jit(solution)/shard_map/dot_general | solution.py:34
  82.7 0.0 copy-start.2
  82.7 7.9 %convolution_convert_fusion = bf16[80,7168]{1,0:T(8,128)(2,1)S(1)} fusion(bf16[1,512,7168]{2,1,0:T(8,128)(2,1)} %param.11, bf16[80,7168]{1,0:T(8,128)(2,1)S(1)} %reshape.34, bf16[1,7168,512]{2,1,0:T(8,128)(2,1)} %param.10, f32[80,512]{1,0:T(8,128)S(1)} %fusion.5), kind=kOutput, calls=%fused_computation.2 | convolution fusion | flops 1175224320 | bytes 17137664 | tf_op jit(solution)/shard_map/dot_general | solution.py:40
  90.7 0.0 copy-start.1
  90.7 29.1 %fusion = bf16[24,7168]{1,0:T(8,128)(2,1)S(1)} fusion(bf16[80,7168]{1,0:T(8,128)(2,1)S(1)} %convolution_convert_fusion), kind=kCustom, calls=%all-reduce-scatter | all-reduce-scatter fusion | flops 688129 | bytes 1491456
  119.8 0.1 slice.9
  119.9 1.9 %collective-permute-start = (bf16[12,7168]{1,0:T(8,128)(2,1)S(1)}, bf16[12,7168]{1,0:T(8,128)(2,1)S(1)}, u32[]{:S(2)}, u32[]{:S(2)}) collective-permute-start(bf16[12,7168]{1,0:T(8,128)(2,1)S(1)} %slice.9), channel_id=1, source_target_pairs={{0,4},{4,8},{8,12},{1,5},{5,9},{9,13},{2,6},{6,10},{10,14},{3,7},{... | collective-permute-start | bytes 516104
  121.7 0.0 copy-done.2
  121.8 0.6 dynamic-slice.4
  123.0 2.3 %collective-permute-done = bf16[12,7168]{1,0:T(8,128)(2,1)S(1)} collective-permute-done((bf16[12,7168]{1,0:T(8,128)(2,1)S(1)}, bf16[12,7168]{1,0:T(8,128)(2,1)S(1)}, u32[]{:S(2)}, u32[]{:S(2)}) %collective-permute-start) | collective-permute-done | bytes 172064
  125.3 2.4 %concatenate = bf16[36,7168]{1,0:T(8,128)(2,1)S(1)} concatenate(bf16[12,7168]{1,0:T(8,128)(2,1)S(1)} %collective-permute-done, bf16[24,7168]{1,0:T(8,128)(2,1)S(1)} %fusion), dimensions={0} | concatenate | bytes 1032192
  127.7 0.1 constant_dynamic-slice_fusion
  127.8 0.9 reshape.35
  128.7 3.5 %all-to-all-start.1 = ((bf16[4,5,7168]{2,1,0:T(8,128)(2,1)}), bf16[4,5,7168]{2,1,0:T(8,128)(2,1)S(1)}, u32[]{:S(2)}, u32[]{:S(2)}) async-start(bf16[4,5,7168]{2,1,0:T(8,128)(2,1)} %reshape.35), calls=%async_computation.1 | async-start | bytes 917504 | tf_op jit(solution)/shard_map/all_to_all | solution.py:46
  132.2 0.0 copy-done
  132.2 0.0 copy-done.1
  132.2 0.1 fusion.22
  132.3 8.0 %all-to-all-done.1 = bf16[4,5,7168]{2,1,0:T(8,128)(2,1)S(1)} async-done(((bf16[4,5,7168]{2,1,0:T(8,128)(2,1)}), bf16[4,5,7168]{2,1,0:T(8,128)(2,1)S(1)}, u32[]{:S(2)}, u32[]{:S(2)}) %all-to-all-start.1) | async-done | bytes 286752 | tf_op jit(solution)/shard_map/all_to_all | solution.py:46
  140.3 4.6 %fusion.1 = bf16[256,7168]{1,0:T(8,128)(2,1)} fusion(bf16[4,5,7168]{2,1,0:T(8,128)(2,1)S(1)} %all-to-all-done.1, f32[256,4]{0,1:T(4,128)S(1)} %fusion.22, s32[256,4]{0,1:T(4,128)S(1)} %convert_subtract_fusion, pred[256,4]{0,1:T(4,128)(4,1)S(1)} %get-tuple-element.5), kind=kOutput, calls=%fused_computation.1 | convolution fusion | flops 442252288 | bytes 3965952 | tf_op jit(solution)/shard_map/dot_general | solution.py:50
  (8 shorter events, 0.1 us)
Async XLA Ops:
  6.5 50.1 %all-gather.3.cloned.1.call-start = ((), (), s32[]{:S(2)}) async-start(), calls=%async_computation.2 | async-start | bytes 2293760 | tf_op jit(solution)/shard_map/all_gather | solution.py:31
  82.7 39.0 %copy-start.2 = (u32[32]{0:T(128)S(1)}, u32[32]{0:T(128)}, u32[]{:S(2)}) copy-start(u32[32]{0:T(128)} %constant.20) | copy-start | bytes 388
  90.7 41.5 %copy-start = (s32[256,8]{0,1:T(8,128)S(1)}, s32[256,8]{0,1:T(8,128)}, u32[]{:S(2)}) copy-start(s32[256,8]{0,1:T(8,128)} %param.7) | copy-start | bytes 24580
  90.7 41.5 %copy-start.1 = (f32[256,8]{0,1:T(8,128)S(1)}, f32[256,8]{0,1:T(8,128)}, u32[]{:S(2)}) copy-start(f32[256,8]{0,1:T(8,128)} %param.8) | copy-start | bytes 24580
  119.9 5.4 %collective-permute-start = (bf16[12,7168]{1,0:T(8,128)(2,1)S(1)}, bf16[12,7168]{1,0:T(8,128)(2,1)S(1)}, u32[]{:S(2)}, u32[]{:S(2)}) collective-permute-start(bf16[12,7168]{1,0:T(8,128)(2,1)S(1)} %slice.9), channel_id=1, source_target_pairs={{0,4},{4,8},{8,12},{1,5},{5,9},{9,13},{2,6},{6,10},{10,14},{3,7},{... | collective-permute-start | bytes 516104
  128.7 11.6 %all-to-all-start.1 = ((bf16[4,5,7168]{2,1,0:T(8,128)(2,1)}), bf16[4,5,7168]{2,1,0:T(8,128)(2,1)S(1)}, u32[]{:S(2)}, u32[]{:S(2)}) async-start(bf16[4,5,7168]{2,1,0:T(8,128)(2,1)} %reshape.35), calls=%async_computation.1 | async-start | bytes 917504 | tf_op jit(solution)/shard_map/all_to_all | solution.py:46
Sparse Core Ops, SparseCore 0:
  12.5 44.0 all-gather.2
where the time goes:
time: 152 us
  waiting for transfers between devices  54.5 us (36%)
  blocking collectives  47.2 us (31%)
  matrix products  20.4 us (13%)
  between operations  14.2 us (9%)
  local copies, waits for them, and re-layouts  7.9 us (5%)
  starting transfers between devices  5.34 us (4%)
  other arithmetic  2.23 us (1%)
    all_gather x1, waiting for transfers between devices, on_device(): gathered = lax.all_gather(send_rows[None], 'node', axis=0, tiled=True)  44.3 us
    unnamed x1, blocking collectives  29.1 us
    all_to_all x1, blocking collectives, on_device(): lax.all_to_all(gathered, 'local', split_axis=1, concat_axis=1, tiled=True)  18.1 us
    all_to_all x1, waiting for transfers between devices, on_device(): lax.all_to_all(expert_out, 'local', split_axis=0, concat_axis=0, tiled=True)  8 us
    dot_general x1, matrix products, on_device(): jnp.dot(flat_act, down_block, preferred_element_type=jnp.float32)  7.92 us
    dot_general x1, matrix products, on_device(): jnp.dot(mixing, returned.reshape(-1, model_width).astype(jnp.float32), pr...  4.58 us
    dot_general x1, matrix products, on_device(): jnp.dot(flat_rows, gate_block, preferred_element_type=jnp.float32)  4.47 us
    all_to_all x1, starting transfers between devices, on_device(): lax.all_to_all(expert_out, 'local', split_axis=0, concat_axis=0, tiled=True)  3.47 us
  transfers between devices with their start and end apart: 3, of which 3 were waited for; matrix products, arithmetic and copies ran while one was open for 0% of the time, Pallas kernels for 0%

commit v1 on v0

v1 whole, which is shorter than its diff:
```python
import functools

import jax
import jax.numpy as jnp
import numpy as np
from jax import lax
from jax.experimental import pallas as pl
from jax.experimental.pallas import tpu as pltpu
from jax.sharding import PartitionSpec as P

EXPERTS = 256
CAP = 5
TILE = 16
FOLD = TILE // CAP
LANE = 128
PARTS = 4
F32 = jnp.float32
BF16 = jnp.bfloat16
MESH = pl.DeviceIdType.MESH


def plan(width):
    tiles = -(-width // (LANE * FOLD))
    base, extra = divmod(tiles, PARTS)
    chunks, off = [], 0
    for c in range(PARTS):
        w = (base + (c < extra)) * LANE
        chunks.append((off, w))
        off += w
    return tiles * LANE, chunks


def piece(width, strip, chunk, k):
    off, w = chunk
    start = k * strip + off
    return start, min(w, width - start)


def unfold_matrix(group):
    m = np.zeros((FOLD * group * CAP, group * TILE), np.float32)
    for k in range(FOLD):
        for s in range(group):
            for i in range(CAP):
                m[k * group * CAP + s * CAP + i, s * TILE + k * CAP + i] = 1
    return m


def expert_kernel(n_node, n_local, group, strip, chunks, hid, ids, rw, unf, fld, gate, up, down, eo, mix, *scratch):
    nc = len(chunks)
    hid_v, gate_v, up_v, down_v = scratch[:4]
    send_a = scratch[4:4 + nc]
    recv_a = scratch[4 + nc:4 + 2 * nc]
    send_b = scratch[4 + 2 * nc:4 + 3 * nc]
    recv_b = scratch[4 + 3 * nc:4 + 4 * nc]
    hid_sem, wt_sem, sa_sem, ra_sem, sb_sem, rb_sem = scratch[4 + 4 * nc:]
    n = n_node * n_local
    node, local = lax.axis_index("node"), lax.axis_index("local")
    me = node * n_local + local
    tokens, width = hid.shape
    rows = n_local * TILE

    def peer_of(d):
        return lax.rem(me + d, n)

    def at(peer):
        return {"node": peer // n_local, "local": lax.rem(peer, n_local)}

    barrier = pltpu.get_barrier_semaphore()

    @pl.loop(1, n)
    def _(d):
        pl.semaphore_signal(barrier, inc=1, device_id=at(peer_of(d)), device_id_type=MESH)

    hid_copies = []
    for c in range(nc):
        for k in range(FOLD):
            start, w = piece(width, strip, chunks[c], k)
            copy = pltpu.make_async_copy(hid.at[:, pl.ds(start, w)], hid_v.at[:, pl.ds(start, w)], hid_sem.at[c, k])
            copy.start()
            hid_copies.append(copy)
    wt_copies = [
        pltpu.make_async_copy(src.at[0], dst, wt_sem.at[j])
        for j, (src, dst) in enumerate(((gate, gate_v), (up, up_v), (down, down_v)))
    ]
    for copy in wt_copies:
        copy.start()

    row = lax.broadcasted_iota(jnp.int32, (rows, tokens), 0)
    want = (row >> 4) * (EXPERTS // n_local)
    low = row & (TILE - 1)
    strip_of = jnp.zeros_like(low)
    for k in range(1, FOLD + 1):
        strip_of += (low >= k * CAP).astype(jnp.int32)
    slot = low - strip_of * CAP
    match = jnp.zeros((rows, tokens), F32)
    share = jnp.zeros((rows, tokens), F32)
    for j in range(ids.shape[0]):
        hit = ids[j:j + 1, :] == want
        match += jnp.where(hit, 1.0, 0.0)
        share += jnp.where(hit, rw[j:j + 1, :], 0.0)
    before = lax.broadcasted_iota(jnp.int32, (tokens, tokens), 0) < lax.broadcasted_iota(jnp.int32, (tokens, tokens), 1)
    position = jnp.dot(match.astype(BF16), before.astype(F32).astype(BF16), preferred_element_type=F32)
    selected = (match > 0.0) & (position == slot.astype(F32))
    sel = [jnp.where(selected & (strip_of == k), 1.0, 0.0).astype(BF16) for k in range(FOLD)]

    def spread(src, dst, s_sem, r_sem, by_expert):
        @pl.loop(1, n)
        def _(d):
            peer = peer_of(d)
            index = lax.rem(peer, n_local) if by_expert else peer
            pltpu.make_async_remote_copy(
                src_ref=src.at[index],
                dst_ref=dst.at[me],
                send_sem=s_sem,
                recv_sem=r_sem,
                device_id=at(peer),
                device_id_type=MESH,
            ).start()

    def drain(ref, sem):
        others = ref.at[pl.ds(0, n - 1)]
        pltpu.make_async_copy(others, others, sem).wait()

    for c in range(nc):
        w_full = chunks[c][1]
        total = None
        for k in range(FOLD):
            hid_copies[c * FOLD + k].wait()
            start, w = piece(width, strip, chunks[c], k)
            part = jnp.dot(sel[k], hid_v[:, start:start + w], preferred_element_type=F32)
            if w < w_full:
                part = jnp.concatenate([part, jnp.zeros((rows, w_full - w), F32)], axis=1)
            total = part if total is None else total + part
        send_a[c][...] = total.astype(BF16).reshape(n_local, TILE, w_full)
        if c == 0:
            pl.semaphore_wait(barrier, n - 1)
        spread(send_a[c], recv_a[c], sa_sem.at[c], ra_sem.at[c], True)
        recv_a[c][me] = send_a[c][local]

    mixed = jnp.where(selected, share, 0.0)
    for k in range(FOLD):
        m = jnp.where(strip_of == k, mixed, 0.0)
        hi = m.astype(BF16).astype(F32)
        mid = (m - hi).astype(BF16).astype(F32)
        lo = m - hi - mid
        mix[k] = jnp.concatenate([hi, mid, lo], axis=0).T.astype(BF16)

    unfold, fold = unf[...], fld[...]
    per = group * CAP
    gate_sum = up_sum = None
    for c in range(nc):
        w_full = chunks[c][1]
        drain(recv_a[c], ra_sem.at[c])
        if c == 0:
            wt_copies[0].wait()
            wt_copies[1].wait()
        flat = [
            jnp.dot(unfold, recv_a[c][g:g + group].reshape(group * TILE, w_full), preferred_element_type=F32).astype(BF16)
            for g in range(0, n, group)
        ]
        for k in range(FOLD):
            start, w = piece(width, strip, chunks[c], k)
            x = [f[k * per:(k + 1) * per, :w] for f in flat]
            x = x[0] if len(x) == 1 else jnp.concatenate(x, axis=0)
            g = jnp.dot(x, gate_v[start:start + w, :], preferred_element_type=F32)
            u = jnp.dot(x, up_v[start:start + w, :], preferred_element_type=F32)
            gate_sum = g if gate_sum is None else gate_sum + g
            up_sum = u if up_sum is None else up_sum + u
    act = (gate_sum / (1.0 + jnp.exp(-gate_sum)) * up_sum).astype(BF16)

    wt_copies[2].wait()
    for c in range(nc):
        w_full = chunks[c][1]
        y = []
        for k in range(FOLD):
            start, w = piece(width, strip, chunks[c], k)
            part = jnp.dot(act, down_v[:, start:start + w], preferred_element_type=F32).astype(BF16)
            if w < w_full:
                part = jnp.concatenate([part, jnp.zeros((part.shape[0], w_full - w), BF16)], axis=1)
            y.append(part)
        for j, g in enumerate(range(0, n, group)):
            stack = jnp.concatenate([p[j * per:(j + 1) * per] for p in y], axis=0)
            folded = jnp.dot(fold, stack, preferred_element_type=F32).astype(BF16)
            send_b[c][g:g + group] = folded.reshape(group, TILE, w_full)
        spread(send_b[c], recv_b[c], sb_sem.at[c], rb_sem.at[c], False)
        recv_b[c][me] = send_b[c][me]

    for c in range(nc):
        off, w_full = chunks[c]
        drain(recv_b[c], rb_sem.at[c])
        total = recv_b[c][0:n_local].astype(F32)
        for z in range(1, n_node):
            total += recv_b[c][z * n_local:(z + 1) * n_local].astype(F32)
        eo[:, off:off + w_full] = total.astype(BF16).reshape(rows, w_full)
    for c in range(nc):
        drain(recv_a[c], sa_sem.at[c])
        drain(recv_b[c], sb_sem.at[c])


def combine_kernel(strip, chunks, eo, mix, out, buf, sems):
    width = out.shape[1]
    copies = []
    for c, (off, w_full) in enumerate(chunks):
        block = eo[:, off:off + w_full]
        block = jnp.concatenate([block, block, block], axis=0)
        for k in range(FOLD):
            start, w = piece(width, strip, chunks[c], k)
            buf[:, start:start + w] = jnp.dot(mix[k], block[:, :w], preferred_element_type=F32).astype(BF16)
            copy = pltpu.make_async_copy(buf.at[:, pl.ds(start, w)], out.at[:, pl.ds(start, w)], sems.at[c, k])
            copy.start()
            copies.append(copy)
    for copy in copies:
        copy.wait()


def on_device(n_node, n_local, hidden_states, expert_ids, route_weights, gate_weight, up_weight, down_weight):
    tokens, width = hidden_states.shape
    units = gate_weight.shape[2]
    n = n_node * n_local
    group = TILE if n % TILE == 0 else n
    strip, chunks = plan(width)
    nc = len(chunks)
    rows = n_local * TILE
    unf = unfold_matrix(group)
    vmem = pl.BlockSpec(memory_space=pltpu.VMEM)
    hbm = pl.BlockSpec(memory_space=pl.ANY)
    eo, mix = pl.pallas_call(
        functools.partial(expert_kernel, n_node, n_local, group, strip, chunks),
        out_shape=[
            jax.ShapeDtypeStruct((rows, strip), BF16),
            jax.ShapeDtypeStruct((FOLD, tokens, 3 * rows), BF16),
        ],
        in_specs=[hbm, vmem, vmem, vmem, vmem, hbm, hbm, hbm],
        out_specs=[vmem, vmem],
        scratch_shapes=[
            pltpu.VMEM((tokens, width), BF16),
            pltpu.VMEM((width, units), BF16),
            pltpu.VMEM((width, units), BF16),
            pltpu.VMEM((units, width), BF16),
            *[pltpu.VMEM((n_local, TILE, w), BF16) for _, w in chunks],
            *[pltpu.VMEM((n, TILE, w), BF16) for _ in range(3) for _, w in chunks],
            pltpu.SemaphoreType.DMA((nc, FOLD)),
            pltpu.SemaphoreType.DMA((3,)),
            *[pltpu.SemaphoreType.DMA((nc,)) for _ in range(4)],
        ],
        compiler_params=pltpu.CompilerParams(
            collective_id=0, has_side_effects=True, vmem_limit_bytes=60 * 1024 * 1024
        ),
    )(
        hidden_states,
        expert_ids.T,
        route_weights.T,
        jnp.asarray(unf, BF16),
        jnp.asarray(unf.T, BF16),
        gate_weight,
        up_weight,
        down_weight,
    )
    return pl.pallas_call(
        functools.partial(combine_kernel, strip, chunks),
        out_shape=jax.ShapeDtypeStruct((tokens, width), BF16),
        in_specs=[vmem, vmem],
        out_specs=hbm,
        scratch_shapes=[pltpu.VMEM((tokens, width), BF16), pltpu.SemaphoreType.DMA((nc, FOLD))],
        compiler_params=pltpu.CompilerParams(vmem_limit_bytes=32 * 1024 * 1024),
    )(eo, mix)


def solution(mesh):
    placed = (
        P(("parts", "node", "local"), None),
        P(("parts", "node", "local"), None),
        P(("parts", "node", "local"), None),
        P("local", None, "node"),
        P("local", None, "node"),
        P("local", "node", None),
    )
    return jax.shard_map(
        functools.partial(on_device, mesh.shape["node"], mesh.shape["local"]),
        mesh=mesh,
        in_specs=placed,
        out_specs=P(("parts", "node", "local"), None),
        check_vma=False,
    )
```

time: 152 us -> 69.2 us (0.46)
  Pallas kernels: 0 us -> 67 us
  waiting for transfers between devices: 54.5 us -> 0 us
  blocking collectives: 47.2 us -> 0 us
  matrix products: 20.4 us -> 0 us
  between operations: 14.2 us -> 0.02 us
  local copies, waits for them, and re-layouts: 7.9 us -> 1.96 us
  starting transfers between devices: 5.34 us -> 0 us
  other arithmetic: 2.23 us -> 0 us
    pallas_call x0 -> x2, Pallas kernels: none -> 67 us  [the longest x1 64.8 us: on_device(): pl.pallas_call(functools.partial(expert_kernel, n_node, n_local, group, s...]
    all_gather x1 -> x0, waiting for transfers between devices: 44.3 us -> none  [on_device(): gathered = lax.all_gather(send_rows[None], 'node', axis=0, tiled=True)]
    unnamed x1 -> x0, blocking collectives: 29.1 us -> none
    dot_general x4 -> x0, matrix products: 20.4 us -> none  [the longest x1 7.92 us: on_device(): jnp.dot(flat_act, down_block, preferred_element_type=jnp.float32)]
    all_to_all x1 -> x0, blocking collectives: 18.1 us -> none  [on_device(): lax.all_to_all(gathered, 'local', split_axis=1, concat_axis=1, tiled=True)]
    all_to_all x1 -> x0, waiting for transfers between devices: 8 us -> none  [on_device(): lax.all_to_all(expert_out, 'local', split_axis=0, concat_axis=0, tiled=True)]
    all_to_all x1 -> x0, starting transfers between devices: 3.47 us -> none  [on_device(): lax.all_to_all(expert_out, 'local', split_axis=0, concat_axis=0, tiled=True)]
    all_gather x1 -> x0, local copies, waits for them, and re-layouts: 2.5 us -> none  [on_device(): gathered = lax.all_gather(send_rows[None], 'node', axis=0, tiled=True)]
  transfers between devices with their start and end apart: 3 -> 0, of which waited for: 3 -> 0; matrix products, arithmetic and copies ran while one was open for 0% -> 0% of each run, Pallas kernels for 0% -> 0%
where the time goes in v1:
time: 69.2 us; the launch traced here: 69 us
  Pallas kernels  67 us (97%)
  local copies, waits for them, and re-layouts  1.96 us (3%)
    pallas_call x1, Pallas kernels, on_device(): pl.pallas_call(functools.partial(expert_kernel, n_node, n_local, group, s...  64.8 us
    pallas_call x1, Pallas kernels, on_device(): pl.pallas_call(functools.partial(combine_kernel, strip, chunks), out_shap...  2.21 us
    unnamed x4, local copies, waits for them, and re-layouts  1.96 us

profile of v1, /device:TPU:0, one launch (start us, length us, event | category | flops | bytes accessed | tf_op | source)
XLA Modules:
  0.0 69.0 jit_solution(6094898712086786229)
XLA Ops:
  0.0 64.8 %shard_map.82 = (bf16[64,2432]{1,0:T(8,128)(2,1)}, bf16[3,256,192]{2,1,0:T(8,128)(2,1)}) custom-call(bf16[256,7168]{1,0:T(8,128)(2,1)} %hid.1, s32[8,256]{1,0:T(8,128)} %bitcast.2, f32[8,256]{1,0:T(8,128)} %bitcast.3, bf16[240,256]{1,0:T(8,128)(2,1)} %constant.4.clone.unf, bf16[256,240]{1,0:T(8,128)(2,1)} %constant.5.clone.fld, bf16[1,7168,512]{2,1,0:T(8,128)(2,1)} %gate.1, ...), custom_call_target="tpu_custom_call" | custom-call | tf_op jit(solution)/shard_map/pallas_call | solution.py:227
  64.8 0.0 copy-start
  64.8 1.0 %copy-done = bf16[3,256,192]{2,1,0:T(8,128)(2,1)S(1)} copy-done((bf16[3,256,192]{2,1,0:T(8,128)(2,1)S(1)}, bf16[3,256,192]{2,1,0:T(8,128)(2,1)}, u32[]{:S(2)}) %copy-start) | copy-done | bytes 294936
  65.8 0.0 copy-start.1
  65.8 1.0 %copy-done.1 = bf16[64,2432]{1,0:T(8,128)(2,1)S(1)} copy-done((bf16[64,2432]{1,0:T(8,128)(2,1)S(1)}, bf16[64,2432]{1,0:T(8,128)(2,1)}, u32[]{:S(2)}) %copy-start.1) | copy-done | bytes 311320
  66.8 2.2 %shard_map.83 = bf16[256,7168]{1,0:T(8,128)(2,1)} custom-call(bf16[64,2432]{1,0:T(8,128)(2,1)S(1)} %copy-done.1, bf16[3,256,192]{2,1,0:T(8,128)(2,1)S(1)} %copy-done), custom_call_target="tpu_custom_call" | custom-call | tf_op jit(solution)/shard_map/pallas_call | solution.py:259
Async XLA Ops:
  64.8 1.0 %copy-start = (bf16[3,256,192]{2,1,0:T(8,128)(2,1)S(1)}, bf16[3,256,192]{2,1,0:T(8,128)(2,1)}, u32[]{:S(2)}) copy-start(bf16[3,256,192]{2,1,0:T(8,128)(2,1)} %get-tuple-element.8.mix) | copy-start | bytes 884740
  65.8 1.0 %copy-start.1 = (bf16[64,2432]{1,0:T(8,128)(2,1)S(1)}, bf16[64,2432]{1,0:T(8,128)(2,1)}, u32[]{:S(2)}) copy-start(bf16[64,2432]{1,0:T(8,128)(2,1)} %get-tuple-element.7.eo) | copy-start | bytes 933892

commit v2 on v1

--- a/solution.py
+++ b/solution.py
@@ -52,24 +52,35 @@
     recv_a = scratch[4 + nc:4 + 2 * nc]
     send_b = scratch[4 + 2 * nc:4 + 3 * nc]
     recv_b = scratch[4 + 3 * nc:4 + 4 * nc]
-    hid_sem, wt_sem, sa_sem, ra_sem, sb_sem, rb_sem = scratch[4 + 4 * nc:]
+    back = scratch[4 + 4 * nc:4 + 5 * nc]
+    (hid_sem, wt_sem, loc_send, loc_recv, in_send, in_recv, out_send, out_recv, back_send, back_recv) = scratch[4 + 5 * nc:]
     n = n_node * n_local
     node, local = lax.axis_index("node"), lax.axis_index("local")
-    me = node * n_local + local
     tokens, width = hid.shape
     rows = n_local * TILE
-
-    def peer_of(d):
-        return lax.rem(me + d, n)
-
-    def at(peer):
-        return {"node": peer // n_local, "local": lax.rem(peer, n_local)}
+    has_left, has_right = node > 0, node < n_node - 1
+    is_first, is_last = node == 0, node == n_node - 1
+    left, right = {"node": node - 1}, {"node": node + 1}
+
+    def plane(ref, s):
+        return ref.at[pl.ds(s * n_local, n_local)]
+
+    def greet(where):
+        pl.semaphore_signal(barrier, inc=1, device_id=where, device_id_type=MESH)
 
     barrier = pltpu.get_barrier_semaphore()
 
-    @pl.loop(1, n)
+    @pl.loop(1, n_local)
     def _(d):
-        pl.semaphore_signal(barrier, inc=1, device_id=at(peer_of(d)), device_id_type=MESH)
+        greet({"local": lax.rem(local + d, n_local)})
+
+    @pl.when(has_left)
+    def _():
+        greet(left)
+
+    @pl.when(has_right)
+    def _():
+        greet(right)
 
     hid_copies = []
     for c in range(nc):
@@ -103,23 +114,45 @@
     selected = (match > 0.0) & (position == slot.astype(F32))
     sel = [jnp.where(selected & (strip_of == k), 1.0, 0.0).astype(BF16) for k in range(FOLD)]
 
-    def spread(src, dst, s_sem, r_sem, by_expert):
-        @pl.loop(1, n)
+    def to_locals(src, base, dst, index, s_sem, r_sem):
+        @pl.loop(1, n_local)
         def _(d):
-            peer = peer_of(d)
-            index = lax.rem(peer, n_local) if by_expert else peer
+            peer = lax.rem(local + d, n_local)
             pltpu.make_async_remote_copy(
-                src_ref=src.at[index],
-                dst_ref=dst.at[me],
+                src_ref=src.at[base + peer],
+                dst_ref=dst.at[index],
                 send_sem=s_sem,
                 recv_sem=r_sem,
-                device_id=at(peer),
+                device_id={"local": peer},
                 device_id_type=MESH,
             ).start()
 
-    def drain(ref, sem):
-        others = ref.at[pl.ds(0, n - 1)]
+    def drain_locals(ref, sem):
+        others = ref.at[pl.ds(0, n_local - 1)]
         pltpu.make_async_copy(others, others, sem).wait()
+
+    def in_copy(c, s, where, way):
+        return pltpu.make_async_remote_copy(
+            src_ref=plane(recv_a[c], s),
+            dst_ref=plane(recv_a[c], s),
+            send_sem=in_send.at[c, s, way],
+            recv_sem=in_recv.at[c, s],
+            device_id=where,
+            device_id_type=MESH,
+        )
+
+    def out_copy(c, s, place, where):
+        return pltpu.make_async_remote_copy(
+            src_ref=plane(send_b[c], s),
+            dst_ref=plane(recv_b[c], place),
+            send_sem=out_send.at[c, s],
+            recv_sem=out_recv.at[c, place],
+            device_id=where,
+            device_id_type=MESH,
+        )
+
+    def arrived(ref, sem):
+        pltpu.make_async_copy(ref, ref, sem).wait()
 
     for c in range(nc):
         w_full = chunks[c][1]
@@ -133,9 +166,20 @@
             total = part if total is None else total + part
         send_a[c][...] = total.astype(BF16).reshape(n_local, TILE, w_full)
         if c == 0:
-            pl.semaphore_wait(barrier, n - 1)
-        spread(send_a[c], recv_a[c], sa_sem.at[c], ra_sem.at[c], True)
-        recv_a[c][me] = send_a[c][local]
+            pl.semaphore_wait(barrier, n_local - 1 + has_left.astype(jnp.int32) + has_right.astype(jnp.int32))
+        to_locals(send_a[c], 0, recv_a[c], node * n_local + local, loc_send.at[c], loc_recv.at[c])
+        recv_a[c][node * n_local + local] = send_a[c][local]
+
+    for c in range(nc):
+        drain_locals(send_a[c], loc_recv.at[c])
+
+        @pl.when(has_right)
+        def _():
+            in_copy(c, node, right, 0).start()
+
+        @pl.when(has_left)
+        def _():
+            in_copy(c, node, left, 1).start()
 
     mixed = jnp.where(selected, share, 0.0)
     for k in range(FOLD):
@@ -145,12 +189,46 @@
         lo = m - hi - mid
         mix[k] = jnp.concatenate([hi, mid, lo], axis=0).T.astype(BF16)
 
+    for c in range(nc):
+        @pl.when(is_first)
+        def _():
+            recv_b[c][0:n_local] = jnp.zeros((n_local, TILE, chunks[c][1]), BF16)
+
+        @pl.when(is_last)
+        def _():
+            recv_b[c][n:n + n_local] = jnp.zeros((n_local, TILE, chunks[c][1]), BF16)
+
+    @pl.loop(1, n_node)
+    def _(h):
+        for c in range(nc):
+            @pl.when((node - h >= 0) & has_right)
+            def _():
+                arrived(plane(recv_a[c], node - h), in_recv.at[c, node - h])
+                in_copy(c, node - h, right, 0).start()
+
+            @pl.when((node + h < n_node) & has_left)
+            def _():
+                arrived(plane(recv_a[c], node + h), in_recv.at[c, node + h])
+                in_copy(c, node + h, left, 1).start()
+
     unfold, fold = unf[...], fld[...]
     per = group * CAP
     gate_sum = up_sum = None
     for c in range(nc):
         w_full = chunks[c][1]
-        drain(recv_a[c], ra_sem.at[c])
+
+        @pl.when(is_last)
+        def _():
+            @pl.loop(0, n_node - 1)
+            def _(s):
+                arrived(plane(recv_a[c], s), in_recv.at[c, s])
+
+        @pl.when(is_first)
+        def _():
+            @pl.loop(1, n_node)
+            def _(s):
+                arrived(plane(recv_a[c], s), in_recv.at[c, s])
+
         if c == 0:
             wt_copies[0].wait()
             wt_copies[1].wait()
@@ -169,7 +247,8 @@
     act = (gate_sum / (1.0 + jnp.exp(-gate_sum)) * up_sum).astype(BF16)
 
     wt_copies[2].wait()
-    for c in range(nc):
+
+    def partial_sums(c):
         w_full = chunks[c][1]
         y = []
         for k in range(FOLD):
@@ -182,19 +261,81 @@
             stack = jnp.concatenate([p[j * per:(j + 1) * per] for p in y], axis=0)
             folded = jnp.dot(fold, stack, preferred_element_type=F32).astype(BF16)
             send_b[c][g:g + group] = folded.reshape(group, TILE, w_full)
-        spread(send_b[c], recv_b[c], sb_sem.at[c], rb_sem.at[c], False)
-        recv_b[c][me] = send_b[c][me]
+
+    def add(c, s):
+        there = pl.ds(s * n_local, n_local)
+        send_b[c][there] = (send_b[c][there].astype(F32) + recv_b[c][there].astype(F32)).astype(BF16)
+
+    for c in range(nc):
+        partial_sums(c)
+
+        @pl.when(is_first)
+        def _():
+            out_copy(c, n_node - 1, n_node - 1, right).start()
+
+        @pl.when(is_last)
+        def _():
+            out_copy(c, 0, lax.select(node == 1, n_node, 0), left).start()
+
+    @pl.loop(0, n_node - 1)
+    def _(e):
+        h = n_node - 1 - e
+        for c in range(nc):
+            @pl.when((node + h < n_node) & (h < n_node - 1))
+            def _():
+                @pl.when(has_left)
+                def _():
+                    arrived(plane(recv_b[c], node + h), out_recv.at[c, node + h])
+                    add(c, node + h)
+
+                out_copy(c, node + h, node + h, right).start()
+
+            @pl.when((node - h >= 0) & (h < n_node - 1))
+            def _():
+                @pl.when(has_right)
+                def _():
+                    arrived(plane(recv_b[c], node - h), out_recv.at[c, node - h])
+                    add(c, node - h)
+
+                out_copy(c, node - h, lax.select(h == 1, n_node, node - h), left).start()
+
+    for c in range(nc):
+        @pl.when(has_left)
+        def _():
+            arrived(plane(recv_b[c], node), out_recv.at[c, node])
+
+        @pl.when(has_right)
+        def _():
+            arrived(plane(recv_b[c], n_node), out_recv.at[c, n_node])
+
+        here = pl.ds(node * n_local, n_local)
+        total = send_b[c][here].astype(F32) + recv_b[c][here].astype(F32) + recv_b[c][n:n + n_local].astype(F32)
+        send_b[c][here] = total.astype(BF16)
+        to_locals(send_b[c], node * n_local, back[c], local, back_send.at[c], back_recv.at[c])
+        back[c][local] = send_b[c][node * n_local + local]
 
     for c in range(nc):
         off, w_full = chunks[c]
-        drain(recv_b[c], rb_sem.at[c])
-        total = recv_b[c][0:n_local].astype(F32)
-        for z in range(1, n_node):
-            total += recv_b[c][z * n_local:(z + 1) * n_local].astype(F32)
-        eo[:, off:off + w_full] = total.astype(BF16).reshape(rows, w_full)
-    for c in range(nc):
-        drain(recv_a[c], sa_sem.at[c])
-        drain(recv_b[c], sb_sem.at[c])
+        drain_locals(send_a[c], back_recv.at[c])
+        eo[:, off:off + w_full] = back[c][...].reshape(rows, w_full)
+
+    for c in range(nc):
+        drain_locals(send_a[c], loc_send.at[c])
+        drain_locals(send_a[c], back_send.at[c])
+
+        @pl.loop(0, n_node)
+        def _(s):
+            @pl.when((s <= node) & has_right)
+            def _():
+                arrived(plane(recv_a[c], s), in_send.at[c, s, 0])
+
+            @pl.when((s >= node) & has_left)
+            def _():
+                arrived(plane(recv_a[c], s), in_send.at[c, s, 1])
+
+            @pl.when(s != node)
+            def _():
+                arrived(plane(send_b[c], s), out_send.at[c, s])
 
 
 def combine_kernel(strip, chunks, eo, mix, out, buf, sems):
@@ -238,10 +379,19 @@
             pltpu.VMEM((width, units), BF16),
             pltpu.VMEM((units, width), BF16),
             *[pltpu.VMEM((n_local, TILE, w), BF16) for _, w in chunks],
-            *[pltpu.VMEM((n, TILE, w), BF16) for _ in range(3) for _, w in chunks],
+            *[pltpu.VMEM((n, TILE, w), BF16) for _ in range(2) for _, w in chunks],
+            *[pltpu.VMEM((n + n_local, TILE, w), BF16) for _, w in chunks],
+            *[pltpu.VMEM((n_local, TILE, w), BF16) for _, w in chunks],
             pltpu.SemaphoreType.DMA((nc, FOLD)),
             pltpu.SemaphoreType.DMA((3,)),
-            *[pltpu.SemaphoreType.DMA((nc,)) for _ in range(4)],
+            pltpu.SemaphoreType.DMA((nc,)),
+            pltpu.SemaphoreType.DMA((nc,)),
+            pltpu.SemaphoreType.DMA((nc, n_node, 2)),
+            pltpu.SemaphoreType.DMA((nc, n_node)),
+            pltpu.SemaphoreType.DMA((nc, n_node)),
+            pltpu.SemaphoreType.DMA((nc, n_node + 1)),
+            pltpu.SemaphoreType.DMA((nc,)),
+            pltpu.SemaphoreType.DMA((nc,)),
         ],
         compiler_params=pltpu.CompilerParams(
             collective_id=0, has_side_effects=True, vmem_limit_bytes=60 * 1024 * 1024

time: 69.2 us -> 61.7 us (0.89)
  Pallas kernels: 67 us -> 59.5 us
    pallas_call x1, Pallas kernels: 64.8 us -> 57.3 us  [on_device(): pl.pallas_call(functools.partial(expert_kernel, n_node, n_local, group, s...]
where the time goes in v2:
time: 61.7 us; the launch traced here: 61.5 us
  Pallas kernels  59.5 us (96%)
  local copies, waits for them, and re-layouts  1.96 us (3%)
    pallas_call x1, Pallas kernels, on_device(): pl.pallas_call(functools.partial(expert_kernel, n_node, n_local, group, s...  57.3 us
    pallas_call x1, Pallas kernels, on_device(): pl.pallas_call(functools.partial(combine_kernel, strip, chunks), out_shap...  2.21 us
    unnamed x4, local copies, waits for them, and re-layouts  1.96 us

profile of v2, /device:TPU:0, one launch (start us, length us, event | category | flops | bytes accessed | tf_op | source)
XLA Modules:
  0.0 61.5 jit_solution(17170799424415027760)
XLA Ops:
  0.0 57.3 %shard_map.82 = (bf16[64,2432]{1,0:T(8,128)(2,1)}, bf16[3,256,192]{2,1,0:T(8,128)(2,1)}) custom-call(bf16[256,7168]{1,0:T(8,128)(2,1)} %hid.1, s32[8,256]{1,0:T(8,128)} %bitcast.2, f32[8,256]{1,0:T(8,128)} %bitcast.3, bf16[240,256]{1,0:T(8,128)(2,1)} %constant.4.clone.unf, bf16[256,240]{1,0:T(8,128)(2,1)} %constant.5.clone.fld, bf16[1,7168,512]{2,1,0:T(8,128)(2,1)} %gate.1, ...), custom_call_target="tpu_custom_call" | custom-call | tf_op jit(solution)/shard_map/pallas_call | solution.py:368
  57.3 0.0 copy-start
  57.3 1.0 %copy-done = bf16[3,256,192]{2,1,0:T(8,128)(2,1)S(1)} copy-done((bf16[3,256,192]{2,1,0:T(8,128)(2,1)S(1)}, bf16[3,256,192]{2,1,0:T(8,128)(2,1)}, u32[]{:S(2)}) %copy-start) | copy-done | bytes 294936
  58.3 0.0 copy-start.1
  58.3 1.0 %copy-done.1 = bf16[64,2432]{1,0:T(8,128)(2,1)S(1)} copy-done((bf16[64,2432]{1,0:T(8,128)(2,1)S(1)}, bf16[64,2432]{1,0:T(8,128)(2,1)}, u32[]{:S(2)}) %copy-start.1) | copy-done | bytes 311320
  59.3 2.2 %shard_map.83 = bf16[256,7168]{1,0:T(8,128)(2,1)} custom-call(bf16[64,2432]{1,0:T(8,128)(2,1)S(1)} %copy-done.1, bf16[3,256,192]{2,1,0:T(8,128)(2,1)S(1)} %copy-done), custom_call_target="tpu_custom_call" | custom-call | tf_op jit(solution)/shard_map/pallas_call | solution.py:409
Async XLA Ops:
  57.3 1.0 %copy-start = (bf16[3,256,192]{2,1,0:T(8,128)(2,1)S(1)}, bf16[3,256,192]{2,1,0:T(8,128)(2,1)}, u32[]{:S(2)}) copy-start(bf16[3,256,192]{2,1,0:T(8,128)(2,1)} %get-tuple-element.8.mix) | copy-start | bytes 884740
  58.3 1.0 %copy-start.1 = (bf16[64,2432]{1,0:T(8,128)(2,1)S(1)}, bf16[64,2432]{1,0:T(8,128)(2,1)}, u32[]{:S(2)}) copy-start(bf16[64,2432]{1,0:T(8,128)(2,1)} %get-tuple-element.7.eo) | copy-start | bytes 933892

commit v3 on v2

--- a/solution.py
+++ b/solution.py
@@ -93,8 +93,6 @@
         pltpu.make_async_copy(src.at[0], dst, wt_sem.at[j])
         for j, (src, dst) in enumerate(((gate, gate_v), (up, up_v), (down, down_v)))
     ]
-    for copy in wt_copies:
-        copy.start()
 
     row = lax.broadcasted_iota(jnp.int32, (rows, tokens), 0)
     want = (row >> 4) * (EXPERTS // n_local)
@@ -181,6 +179,9 @@
         def _():
             in_copy(c, node, left, 1).start()
 
+    for copy in wt_copies:
+        copy.start()
+
     mixed = jnp.where(selected, share, 0.0)
     for k in range(FOLD):
         m = jnp.where(strip_of == k, mixed, 0.0)
@@ -338,8 +339,16 @@
                 arrived(plane(send_b[c], s), out_send.at[c, s])
 
 
-def combine_kernel(strip, chunks, eo, mix, out, buf, sems):
+def combine_kernel(strip, chunks, eo_hbm, mix_hbm, out, eo, mix, buf, in_sems, sems):
     width = out.shape[1]
+    loads = [
+        pltpu.make_async_copy(src, dst, in_sems.at[j])
+        for j, (src, dst) in enumerate(((eo_hbm, eo), (mix_hbm, mix)))
+    ]
+    for copy in loads:
+        copy.start()
+    for copy in loads:
+        copy.wait()
     copies = []
     for c, (off, w_full) in enumerate(chunks):
         block = eo[:, off:off + w_full]
@@ -409,10 +418,16 @@
     return pl.pallas_call(
         functools.partial(combine_kernel, strip, chunks),
         out_shape=jax.ShapeDtypeStruct((tokens, width), BF16),
-        in_specs=[vmem, vmem],
+        in_specs=[hbm, hbm],
         out_specs=hbm,
-        scratch_shapes=[pltpu.VMEM((tokens, width), BF16), pltpu.SemaphoreType.DMA((nc, FOLD))],
-        compiler_params=pltpu.CompilerParams(vmem_limit_bytes=32 * 1024 * 1024),
+        scratch_shapes=[
+            pltpu.VMEM((rows, strip), BF16),
+            pltpu.VMEM((FOLD, tokens, 3 * rows), BF16),
+            pltpu.VMEM((tokens, width), BF16),
+            pltpu.SemaphoreType.DMA((2,)),
+            pltpu.SemaphoreType.DMA((nc, FOLD)),
+        ],
+        compiler_params=pltpu.CompilerParams(vmem_limit_bytes=60 * 1024 * 1024),
     )(eo, mix)
 
 

time: 61.7 us -> 59.9 us (0.971); the launches traced: 61.5 us -> 58.8 us
  local copies, waits for them, and re-layouts: 1.96 us -> 0 us
  Pallas kernels: 59.5 us -> 58.8 us
    unnamed x4 -> x0, local copies, waits for them, and re-layouts: 1.96 us -> none
    pallas_call x1, Pallas kernels: 57.3 us -> 55.5 us  [on_device(): pl.pallas_call(functools.partial(expert_kernel, n_node, n_local, group, s...]
    pallas_call x1, Pallas kernels: 2.21 us -> 3.34 us  [on_device(): pl.pallas_call(functools.partial(combine_kernel, strip, chunks), out_shap...]
where the time goes in v3:
time: 59.9 us; the launch traced here: 58.8 us
  Pallas kernels  58.8 us (98%)
    pallas_call x1, Pallas kernels, on_device(): pl.pallas_call(functools.partial(expert_kernel, n_node, n_local, group, s...  55.5 us
    pallas_call x1, Pallas kernels, on_device(): pl.pallas_call(functools.partial(combine_kernel, strip, chunks), out_shap...  3.34 us

profile of v3, /device:TPU:0, one launch (start us, length us, event | category | flops | bytes accessed | tf_op | source)
XLA Modules:
  0.0 58.8 jit_solution(1666379069115034409)
XLA Ops:
  0.0 55.5 %shard_map.82 = (bf16[64,2432]{1,0:T(8,128)(2,1)}, bf16[3,256,192]{2,1,0:T(8,128)(2,1)}) custom-call(bf16[256,7168]{1,0:T(8,128)(2,1)} %hid.1, s32[8,256]{1,0:T(8,128)} %bitcast.2, f32[8,256]{1,0:T(8,128)} %bitcast.3, bf16[240,256]{1,0:T(8,128)(2,1)} %constant.4.clone.unf, bf16[256,240]{1,0:T(8,128)(2,1)} %constant.5.clone.fld, bf16[1,7168,512]{2,1,0:T(8,128)(2,1)} %gate.1, ...), custom_call_target="tpu_custom_call" | custom-call | tf_op jit(solution)/shard_map/pallas_call | solution.py:377
  55.5 3.3 %shard_map.83 = bf16[256,7168]{1,0:T(8,128)(2,1)} custom-call(bf16[64,2432]{1,0:T(8,128)(2,1)} %get-tuple-element.7.eo_hbm, bf16[3,256,192]{2,1,0:T(8,128)(2,1)} %get-tuple-element.8.mix_hbm), custom_call_target="tpu_custom_call" | custom-call | tf_op jit(solution)/shard_map/pallas_call | solution.py:418

commit v4 on v3

--- a/solution.py
+++ b/solution.py
@@ -199,76 +199,120 @@
         def _():
             recv_b[c][n:n + n_local] = jnp.zeros((n_local, TILE, chunks[c][1]), BF16)
 
-    @pl.loop(1, n_node)
-    def _(h):
-        for c in range(nc):
-            @pl.when((node - h >= 0) & has_right)
-            def _():
-                arrived(plane(recv_a[c], node - h), in_recv.at[c, node - h])
-                in_copy(c, node - h, right, 0).start()
-
-            @pl.when((node + h < n_node) & has_left)
-            def _():
-                arrived(plane(recv_a[c], node + h), in_recv.at[c, node + h])
-                in_copy(c, node + h, left, 1).start()
-
+    half_planes = n_node // 2
+    half = half_planes * n_local
+    near_plane = lax.select(node < half_planes, 0, half_planes)
+    far_plane = half_planes - near_plane
     unfold, fold = unf[...], fld[...]
     per = group * CAP
-    gate_sum = up_sum = None
-    for c in range(nc):
-        w_full = chunks[c][1]
-
-        @pl.when(is_last)
-        def _():
-            @pl.loop(0, n_node - 1)
+
+    def pass_on(c, h):
+        @pl.when((node - h >= 0) & has_right)
+        def _():
+            arrived(plane(recv_a[c], node - h), in_recv.at[c, node - h])
+            in_copy(c, node - h, right, 0).start()
+
+        @pl.when((node + h < n_node) & has_left)
+        def _():
+            arrived(plane(recv_a[c], node + h), in_recv.at[c, node + h])
+            in_copy(c, node + h, left, 1).start()
+
+    def await_planes(c, first, last):
+        @pl.when(is_first)
+        def _():
+            @pl.loop(*first)
             def _(s):
                 arrived(plane(recv_a[c], s), in_recv.at[c, s])
 
-        @pl.when(is_first)
-        def _():
-            @pl.loop(1, n_node)
+        @pl.when(is_last)
+        def _():
+            @pl.loop(*last)
             def _(s):
                 arrived(plane(recv_a[c], s), in_recv.at[c, s])
 
-        if c == 0:
-            wt_copies[0].wait()
-            wt_copies[1].wait()
+    def project(c, base, sums):
+        w_full = chunks[c][1]
         flat = [
-            jnp.dot(unfold, recv_a[c][g:g + group].reshape(group * TILE, w_full), preferred_element_type=F32).astype(BF16)
-            for g in range(0, n, group)
+            jnp.dot(
+                unfold,
+                recv_a[c][pl.ds(base + g, group)].reshape(group * TILE, w_full),
+                preferred_element_type=F32,
+            )
+            for g in range(0, half, group)
         ]
         for k in range(FOLD):
             start, w = piece(width, strip, chunks[c], k)
             x = [f[k * per:(k + 1) * per, :w] for f in flat]
-            x = x[0] if len(x) == 1 else jnp.concatenate(x, axis=0)
+            x = (x[0] if len(x) == 1 else jnp.concatenate(x, axis=0)).astype(BF16)
             g = jnp.dot(x, gate_v[start:start + w, :], preferred_element_type=F32)
             u = jnp.dot(x, up_v[start:start + w, :], preferred_element_type=F32)
-            gate_sum = g if gate_sum is None else gate_sum + g
-            up_sum = u if up_sum is None else up_sum + u
-    act = (gate_sum / (1.0 + jnp.exp(-gate_sum)) * up_sum).astype(BF16)
-
-    wt_copies[2].wait()
-
-    def partial_sums(c):
+            sums = (g, u) if sums is None else (sums[0] + g, sums[1] + u)
+        return sums
+
+    def activate(sums):
+        return (sums[0] / (1.0 + jnp.exp(-sums[0])) * sums[1]).astype(BF16)
+
+    def partial_sums(c, base, act):
         w_full = chunks[c][1]
         y = []
         for k in range(FOLD):
             start, w = piece(width, strip, chunks[c], k)
-            part = jnp.dot(act, down_v[:, start:start + w], preferred_element_type=F32).astype(BF16)
+            part = jnp.dot(act, down_v[:, start:start + w], preferred_element_type=F32)
             if w < w_full:
-                part = jnp.concatenate([part, jnp.zeros((part.shape[0], w_full - w), BF16)], axis=1)
+                part = jnp.concatenate([part, jnp.zeros((part.shape[0], w_full - w), F32)], axis=1)
             y.append(part)
-        for j, g in enumerate(range(0, n, group)):
-            stack = jnp.concatenate([p[j * per:(j + 1) * per] for p in y], axis=0)
+        for j, g in enumerate(range(0, half, group)):
+            stack = jnp.concatenate([p[j * per:(j + 1) * per] for p in y], axis=0).astype(BF16)
             folded = jnp.dot(fold, stack, preferred_element_type=F32).astype(BF16)
-            send_b[c][g:g + group] = folded.reshape(group, TILE, w_full)
+            send_b[c][pl.ds(base + g, group)] = folded.reshape(group, TILE, w_full)
+
+    @pl.loop(1, half_planes)
+    def _(h):
+        for c in range(nc):
+            pass_on(c, h)
+
+    sums = None
+    for c in range(nc):
+        await_planes(c, (1, half_planes), (half_planes, n_node - 1))
+        if c == 0:
+            wt_copies[0].wait()
+            wt_copies[1].wait()
+        sums = project(c, near_plane * n_local, sums)
+
+        @pl.loop(half_planes, n_node)
+        def _(h):
+            pass_on(c, h)
+
+    act = activate(sums)
+    wt_copies[2].wait()
+    for c in range(nc):
+        partial_sums(c, near_plane * n_local, act)
+
+        @pl.when(is_first)
+        def _():
+            @pl.loop(1, half_planes)
+            def _(e):
+                s = half_planes - e
+                out_copy(c, s, s, right).start()
+
+        @pl.when(is_last)
+        def _():
+            @pl.loop(half_planes, n_node - 1)
+            def _(s):
+                out_copy(c, s, lax.select(node - s == 1, n_node, s), left).start()
+
+    sums = None
+    for c in range(nc):
+        await_planes(c, (half_planes, n_node), (0, half_planes))
+        sums = project(c, far_plane * n_local, sums)
+    act = activate(sums)
 
     def add(c, s):
         there = pl.ds(s * n_local, n_local)
         send_b[c][there] = (send_b[c][there].astype(F32) + recv_b[c][there].astype(F32)).astype(BF16)
 
     for c in range(nc):
-        partial_sums(c)
+        partial_sums(c, far_plane * n_local, act)
 
         @pl.when(is_first)
         def _():
@@ -282,7 +326,7 @@
     def _(e):
         h = n_node - 1 - e
         for c in range(nc):
-            @pl.when((node + h < n_node) & (h < n_node - 1))
+            @pl.when((node + h < n_node) & (h < n_node - 1) & (has_left | (h >= half_planes)))
             def _():
                 @pl.when(has_left)
                 def _():
@@ -291,7 +335,7 @@
 
                 out_copy(c, node + h, node + h, right).start()
 
-            @pl.when((node - h >= 0) & (h < n_node - 1))
+            @pl.when((node - h >= 0) & (h < n_node - 1) & (has_right | (h >= half_planes)))
             def _():
                 @pl.when(has_right)
                 def _():
@@ -367,7 +411,8 @@
     tokens, width = hidden_states.shape
     units = gate_weight.shape[2]
     n = n_node * n_local
-    group = TILE if n % TILE == 0 else n
+    half = n // 2
+    group = TILE if half % TILE == 0 else half
     strip, chunks = plan(width)
     nc = len(chunks)
     rows = n_local * TILE

time: 59.9 us -> 58.6 us (0.978); the launches traced: 58.8 us -> 58.4 us
  no operation moved by 1% of the time
where the time goes in v4:
time: 58.6 us; the launch traced here: 58.4 us
  Pallas kernels  58.4 us (100%)
    pallas_call x1, Pallas kernels, on_device(): pl.pallas_call(functools.partial(expert_kernel, n_node, n_local, group, s...  55 us
    pallas_call x1, Pallas kernels, on_device(): pl.pallas_call(functools.partial(combine_kernel, strip, chunks), out_shap...  3.35 us

profile of v4, /device:TPU:0, one launch (start us, length us, event | category | flops | bytes accessed | tf_op | source)
XLA Modules:
  0.0 58.4 jit_solution(15720539899825252701)
XLA Ops:
  0.0 55.0 %shard_map.82 = (bf16[64,2432]{1,0:T(8,128)(2,1)}, bf16[3,256,192]{2,1,0:T(8,128)(2,1)}) custom-call(bf16[256,7168]{1,0:T(8,128)(2,1)} %hid.1, s32[8,256]{1,0:T(8,128)} %bitcast.2, f32[8,256]{1,0:T(8,128)} %bitcast.3, bf16[120,128]{1,0:T(8,128)(2,1)} %constant.4.clone.unf, bf16[128,120]{1,0:T(8,128)(2,1)} %constant.5.clone.fld, bf16[1,7168,512]{2,1,0:T(8,128)(2,1)} %gate.1, ...), custom_call_target="tpu_custom_call" | custom-call | tf_op jit(solution)/shard_map/pallas_call | solution.py:422
  55.1 3.3 %shard_map.83 = bf16[256,7168]{1,0:T(8,128)(2,1)} custom-call(bf16[64,2432]{1,0:T(8,128)(2,1)} %get-tuple-element.7.eo_hbm, bf16[3,256,192]{2,1,0:T(8,128)(2,1)} %get-tuple-element.8.mix_hbm), custom_call_target="tpu_custom_call" | custom-call | tf_op jit(solution)/shard_map/pallas_call | solution.py:463

commit v5 on v4

--- a/solution.py
+++ b/solution.py
@@ -13,7 +13,7 @@
 TILE = 16
 FOLD = TILE // CAP
 LANE = 128
-PARTS = 4
+PARTS = 6
 F32 = jnp.float32
 BF16 = jnp.bfloat16
 MESH = pl.DeviceIdType.MESH

time: 58.6 us -> 57.9 us (0.988)
  Pallas kernels: 58.4 us -> 57.7 us
    pallas_call x1, Pallas kernels: 55 us -> 54.1 us  [on_device(): pl.pallas_call(functools.partial(expert_kernel, n_node, n_local, group, s...]
where the time goes in v5:
time: 57.9 us; the launch traced here: 57.7 us
  Pallas kernels  57.7 us (100%)
    pallas_call x1, Pallas kernels, on_device(): pl.pallas_call(functools.partial(expert_kernel, n_node, n_local, group, s...  54.1 us
    pallas_call x1, Pallas kernels, on_device(): pl.pallas_call(functools.partial(combine_kernel, strip, chunks), out_shap...  3.61 us

profile of v5, /device:TPU:0, one launch (start us, length us, event | category | flops | bytes accessed | tf_op | source)
XLA Modules:
  0.0 57.7 jit_solution(6318085806965318527)
XLA Ops:
  0.0 54.1 %shard_map.82 = (bf16[64,2432]{1,0:T(8,128)(2,1)}, bf16[3,256,192]{2,1,0:T(8,128)(2,1)}) custom-call(bf16[256,7168]{1,0:T(8,128)(2,1)} %hid.1, s32[8,256]{1,0:T(8,128)} %bitcast.2, f32[8,256]{1,0:T(8,128)} %bitcast.3, bf16[120,128]{1,0:T(8,128)(2,1)} %constant.4.clone.unf, bf16[128,120]{1,0:T(8,128)(2,1)} %constant.5.clone.fld, bf16[1,7168,512]{2,1,0:T(8,128)(2,1)} %gate.1, ...), custom_call_target="tpu_custom_call" | custom-call | tf_op jit(solution)/shard_map/pallas_call | solution.py:422
  54.1 3.6 %shard_map.83 = bf16[256,7168]{1,0:T(8,128)(2,1)} custom-call(bf16[64,2432]{1,0:T(8,128)(2,1)} %get-tuple-element.7.eo_hbm, bf16[3,256,192]{2,1,0:T(8,128)(2,1)} %get-tuple-element.8.mix_hbm), custom_call_target="tpu_custom_call" | custom-call | tf_op jit(solution)/shard_map/pallas_call | solution.py:463
